TPU v7x, 128 devices: a whole 4x4x4 slice. The times are simulated.
128 devices in a mesh: dp: 4 (over z), mp: 32 (over x, y, core).
Axes of the slice: x: 4, y: 4, z: 4, core: 2. Of those that a mesh axis runs over, the one named last changes fastest.
Arguments:
- tokens: bfloat16 [16384, 4096], P(('dp', 'mp')), may hold values from -6 to 6
- expert_ids: int32 [16384, 1], P(('dp', 'mp')), may hold values from 0 to 63; in each aligned block of 128 rows (0 to 127, 128 to 255, ...) at most 3 rows name the same one
- gate_probs: float32 [16384, 1], P(('dp', 'mp')), may hold values from 0.3 to 1
- gate_weight: bfloat16 [64, 4096, 1536], P('mp', None, 'dp'), may hold values from -0.09375 to 0.09375
- up_weight: bfloat16 [64, 4096, 1536], P('mp', None, 'dp'), may hold values from -0.09375 to 0.09375
- down_weight: bfloat16 [64, 1536, 4096], P('mp', 'dp'), may hold values from -0.15625 to 0.15625
- sign_offset: int32 [1], replicated, may hold values from 1 to 999999999
Outputs:
- out_plus: bfloat16 [16384, 4096], P(('dp', 'mp'))
- out_minus: bfloat16 [16384, 4096], P(('dp', 'mp'))
Inputs may be any that keep to these rules, and one draw needn't show every extreme that they name: `expert_ids`: within each aligned block of 128 tokens (the tokens of one device) no expert is named by more than 3 routes, a bound that some block reaches.
All inputs are finite; a program needn't handle non-finite values.
Results may differ from a plain program's by a relative error of at most 0.01.
Values may be sent and summed in bfloat16 or wider, within the bound.
A program may use at most 128 MiB of HBM per device.

v0:
```python
import jax
import jax.numpy as jnp
from jax import lax
from jax.sharding import PartitionSpec as P

FF = 1536
epsilon_step = 0.005


def mixing(number):
    number = number ^ lax.shift_right_logical(number, jnp.full_like(number, 16))
    number = number * 73244475
    number = number ^ lax.shift_right_logical(number, jnp.full_like(number, 16))
    number = number * 73244475
    return number ^ lax.shift_right_logical(number, jnp.full_like(number, 16))


def sign_noise(offset_mixed, position, matrix_tag):
    hashed = mixing(position * 3 + matrix_tag ^ offset_mixed)
    parity = lax.shift_right_logical(hashed, jnp.full_like(hashed, 9)) & 1
    return (parity * 2 - 1).astype(jnp.float32)


def perturb(weight, noise, direction):
    return (weight.astype(jnp.float32) + direction * epsilon_step * noise).astype(jnp.bfloat16)


def expert_rows(arrived, weight_sets):
    lead_shape = arrived.shape
    model_width = lead_shape[-1]
    per_expert = []
    for local_expert in range(lead_shape[2]):
        flat_rows = arrived[:, :, local_expert].reshape(-1, model_width)
        by_pass = []
        for gate_moved, up_moved, down_moved in weight_sets[local_expert]:
            gate_act = jnp.dot(flat_rows, gate_moved, preferred_element_type=jnp.float32)
            up_act = jnp.dot(flat_rows, up_moved, preferred_element_type=jnp.float32)
            hidden = (jax.nn.silu(gate_act) * up_act).astype(jnp.bfloat16)
            by_pass.append(
                jnp.dot(hidden, down_moved, preferred_element_type=jnp.float32).astype(jnp.bfloat16)
            )
        stacked = jnp.stack(by_pass, axis=1).reshape(
            lead_shape[0], lead_shape[1], lead_shape[3], len(by_pass), model_width
        )
        per_expert.append(stacked)
    return jnp.stack(per_expert, axis=2)


def shards(tokens, expert_ids, gate_probs, gate_weight, up_weight, down_weight, sign_offset):
    mp_count = lax.axis_size("mp")
    tok_rows, model_width = tokens.shape
    route_count = expert_ids.shape[1]
    local_count = gate_weight.shape[0]
    quarter = gate_weight.shape[2]
    expert_count = local_count * mp_count
    capacity = 3 * tok_rows * route_count // (2 * expert_count)
    offset_mixed = mixing(sign_offset[0] * 668265261 + 12345)
    expert_base = lax.axis_index("mp") * local_count
    hidden_base = lax.axis_index("dp") * quarter
    width_axis = lax.broadcasted_iota(jnp.int32, (model_width, quarter), 0)
    unit_axis = lax.broadcasted_iota(jnp.int32, (model_width, quarter), 1) + hidden_base
    plus_sets = []
    minus_sets = []
    for local_expert in range(local_count):
        expert_global = expert_base + local_expert
        gate_pos = (expert_global * model_width + width_axis) * FF + unit_axis
        down_pos = (expert_global * FF + unit_axis.T) * model_width + width_axis.T
        noise_gate = sign_noise(offset_mixed, gate_pos, 0)
        noise_up = sign_noise(offset_mixed, gate_pos, 1)
        noise_down = sign_noise(offset_mixed, down_pos, 2)
        for direction, target in ((1.0, plus_sets), (-1.0, minus_sets)):
            target.append(
                (
                    perturb(gate_weight[local_expert], noise_gate, direction),
                    perturb(up_weight[local_expert], noise_up, direction),
                    perturb(down_weight[local_expert], noise_down, direction),
                )
            )
    route_flat = expert_ids.reshape(-1)
    expert_axis = lax.broadcasted_iota(jnp.int32, (route_flat.shape[0], expert_count), 1)
    onehot = (route_flat[:, None] == expert_axis).astype(jnp.int32)
    earlier = jnp.cumsum(onehot, axis=0, dtype=jnp.int32) - onehot
    rank_in = jnp.sum(earlier * onehot, axis=1, dtype=jnp.int32)
    slot_of = (route_flat * capacity + rank_in).reshape(tok_rows, route_count)
    slot_axis = lax.broadcasted_iota(jnp.int32, (expert_count * capacity, tok_rows), 0)
    selector = (slot_axis == slot_of[:, 0][None, :]).astype(jnp.float32)
    outgoing = jnp.dot(
        selector.astype(jnp.bfloat16), tokens, preferred_element_type=jnp.float32
    ).astype(jnp.bfloat16)
    outgoing = outgoing.reshape(mp_count, local_count, capacity, model_width)
    grouped = lax.all_gather(outgoing[None], "dp", axis=0, tiled=True)
    arrived = lax.all_to_all(grouped, "mp", split_axis=1, concat_axis=1, tiled=True)

    def finish(weight_sets):
        partials = expert_rows(arrived, weight_sets)
        returned = lax.all_to_all(partials, "mp", split_axis=1, concat_axis=1, tiled=True)
        summed = lax.psum_scatter(
            returned.astype(jnp.float32).astype(jnp.bfloat16), "dp", scatter_dimension=0, tiled=True
        ).astype(jnp.float32)
        return summed[0].astype(jnp.bfloat16)

    def combine(result, pass_index):
        flat_out = result.reshape(expert_count * capacity, result.shape[3], model_width)[
            :, pass_index
        ]
        picked = (
            jnp.take(flat_out, slot_of.reshape(-1), axis=0)
            .reshape(tok_rows, route_count, model_width)
            .astype(jnp.float32)
        )
        return jnp.sum(gate_probs[:, :, None] * picked, axis=1).astype(jnp.bfloat16)

    plus_result = finish([[entry_set] for entry_set in plus_sets])
    minus_result = finish([[entry_set] for entry_set in minus_sets])
    return (combine(plus_result, 0), combine(minus_result, 0))


def solution(mesh):
    in_specs = (
        P(("dp", "mp"), None),
        P(("dp", "mp"), None),
        P(("dp", "mp"), None),
        P("mp", None, "dp"),
        P("mp", None, "dp"),
        P("mp", "dp", None),
        P(),
    )
    out_specs = (P(("dp", "mp"), None), P(("dp", "mp"), None))
    return jax.shard_map(shards, mesh=mesh, in_specs=in_specs, out_specs=out_specs, check_vma=False)
```

profile of v0, /device:TPU:1, one launch (start us, length us, event | category | flops | bytes accessed | tf_op | source)
XLA Modules:
  0.0 660.6 jit_solution(3425733113894375996)
XLA Ops:
  17.6 69.3 %all-gather.2.cloned.1.call-done = bf16[4,32,2,3,4096]{4,1,3,2,0:T(8,128)(2,1)} async-done(((bf16[1,32,2,3,4096]{4,1,3,2,0:T(8,128)(2,1)}), bf16[4,32,2,3,4096]{4,1,3,2,0:T(8,128)(2,1)}) %all-gather.2.cloned.1.call-update) | async-done | bytes 6291472 | tf_op jit(solution)/shard_map/all_gather | solution.py:91
  86.8 10.3 %copy.14 = bf16[4,32,2,3,4096]{4,0,3,2,1:T(4,128)(2,1)} copy(bf16[4,32,2,3,4096]{4,1,3,2,0:T(8,128)(2,1)} %all-gather.2.cloned.1.call-done) | data formatting | bytes 12582912 | tf_op jit(solution)/shard_map/all_gather | solution.py:91
  97.1 7.6 %all-to-all-start = ((bf16[4,32,2,3,4096]{4,0,3,2,1:T(4,128)(2,1)}), bf16[4,32,2,3,4096]{4,0,3,2,1:T(4,128)(2,1)}, u32[]{:S(2)}, u32[]{:S(2)}) async-start(bf16[4,32,2,3,4096]{4,0,3,2,1:T(4,128)(2,1)} %copy.14), calls=%async_computation | async-start | bytes 12582912 | tf_op jit(solution)/shard_map/all_to_all | solution.py:92
  105.7 77.0 %all-to-all-done = bf16[4,32,2,3,4096]{4,0,3,2,1:T(4,128)(2,1)} async-done(((bf16[4,32,2,3,4096]{4,0,3,2,1:T(4,128)(2,1)}), bf16[4,32,2,3,4096]{4,0,3,2,1:T(4,128)(2,1)}, u32[]{:S(2)}, u32[]{:S(2)}) %all-to-all-start) | async-done | bytes 6291488 | tf_op jit(solution)/shard_map/all_to_all | solution.py:92
  182.7 6.9 %fusion.296 = (bf16[4,32,1,3,4096]{4,0,3,2,1:T(4,128)(2,1)}, bf16[4,32,1,3,4096]{4,0,3,2,1:T(4,128)(2,1)S(1)}) fusion(bf16[4,32,2,3,4096]{4,0,3,2,1:T(4,128)(2,1)} %all-to-all-done), kind=kLoop, calls=%fused_computation.284 | loop fusion | bytes 12582912 | tf_op jit(solution)/shard_map/slice | solution.py:33
  189.6 4.6 copy.16
  194.3 7.4 %reshape_squeeze.9 = bf16[384,4096]{1,0:T(8,128)(2,1)} reshape(bf16[4,32,1,3,4096]{4,3,1,0,2:T(4,128)(2,1)} %copy.16) | data formatting | bytes 6291456 | tf_op jit(solution)/shard_map/reshape;squeeze | solution.py:33
  201.7 7.5 %fusion.118 = f32[384,384]{1,0:T(8,128)S(1)} fusion(bf16[384,4096]{1,0:T(8,128)(2,1)} %reshape_squeeze.9, s32[4096]{0:T(1024)S(1)} %add_multiply_fusion.2, s32[]{:T(128)S(6)} %xor.269, s32[384]{0:T(512)S(1)} %iota_add_fusion, bf16[2,4096,384]{2,1,0:T(8,128)(2,1)} %param.12), kind=kOutput, calls=%fused_computation.151 | convolution fusion | flops 1239416832 | bytes 6899204 | tf_op jit(solution)/shard_map/dot_general | solution.py:36
  209.2 15.7 %convolution_convert_fusion.2 = bf16[384,4096]{1,0:T(8,128)(2,1)} fusion(s32[384]{0:T(512)S(1)} %get-tuple-element.9, s32[]{:T(128)S(6)} %xor.269, bf16[2,384,4096]{2,1,0:T(8,128)(2,1)} %param.14, bf16[384,4096]{1,0:T(8,128)(2,1)} %reshape_squeeze.9, s32[4096]{0:T(1024)S(1)} %add_multiply_fusion.2, s32[384]{0:T(512)S(1)} %iota_add_fusion, ...), kind=kOutput, calls=%fused_computation.92 | convolution fusion | flops 2484436992 | bytes 13193216 | tf_op jit(solution)/shard_map/dot_general | solution.py:40
  224.9 7.1 %stack_reshape_stack.13 = bf16[4,32,1,3,1,4096]{5,3,1,0,4,2:T(4,128)(2,1)} reshape(bf16[384,4096]{1,0:T(8,128)(2,1)} %convolution_convert_fusion.2) | data formatting | bytes 6291456 | tf_op jit(solution)/shard_map/stack;reshape;stack | solution.py:46
  232.0 7.4 %copy.15 = bf16[4,32,1,3,4096]{4,3,1,0,2:T(4,128)(2,1)} copy(bf16[4,32,1,3,4096]{4,0,3,2,1:T(4,128)(2,1)} %get-tuple-element.5) | data formatting | bytes 6291456 | tf_op jit(solution)/shard_map/slice | solution.py:33
  239.4 7.4 %reshape_squeeze.8 = bf16[384,4096]{1,0:T(8,128)(2,1)} reshape(bf16[4,32,1,3,4096]{4,3,1,0,2:T(4,128)(2,1)} %copy.15) | data formatting | bytes 6291456 | tf_op jit(solution)/shard_map/reshape;squeeze | solution.py:33
  246.8 7.5 %fusion.110 = f32[384,384]{1,0:T(8,128)S(1)} fusion(bf16[384,4096]{1,0:T(8,128)(2,1)} %reshape_squeeze.8, s32[]{:T(128)S(6)} %xor.269, s32[384]{0:T(512)S(1)} %iota_add_fusion, s32[4096]{0:T(1024)S(1)} %add_multiply_fusion.3, bf16[2,4096,384]{2,1,0:T(8,128)(2,1)} %param.12), kind=kOutput, calls=%fused_computation.147 | convolution fusion | flops 1239416832 | bytes 6899204 | tf_op jit(solution)/shard_map/dot_general | solution.py:36
  254.3 15.5 %convolution_convert_fusion.3 = bf16[384,4096]{1,0:T(8,128)(2,1)} fusion(s32[]{:T(128)S(6)} %xor.269, s32[384]{0:T(512)S(1)} %get-tuple-element.10, bf16[2,384,4096]{2,1,0:T(8,128)(2,1)} %param.14, bf16[384,4096]{1,0:T(8,128)(2,1)} %reshape_squeeze.8, s32[384]{0:T(512)S(1)} %iota_add_fusion, s32[4096]{0:T(1024)S(1)} %add_multiply_fusion.3, ...), kind=kOutput, calls=%fused_computation.93 | convolution fusion | flops 2484436992 | bytes 13193216 | tf_op jit(solution)/shard_map/dot_general | solution.py:40
  269.8 7.1 %stack_reshape_stack.12 = bf16[4,32,1,3,1,4096]{5,3,1,0,4,2:T(4,128)(2,1)} reshape(bf16[384,4096]{1,0:T(8,128)(2,1)} %convolution_convert_fusion.3) | data formatting | bytes 6291456 | tf_op jit(solution)/shard_map/stack;reshape;stack | solution.py:46
  276.9 8.7 %pad_maximum_fusion = bf16[4,32,2,3,1,4096]{5,3,1,0,4,2:T(4,128)(2,1)} fusion(bf16[4,32,1,3,1,4096]{5,3,1,0,4,2:T(4,128)(2,1)} %stack_reshape_stack.13, bf16[4,32,1,3,1,4096]{5,3,1,0,4,2:T(4,128)(2,1)} %stack_reshape_stack.12), kind=kLoop, calls=%fused_computation.20 | loop fusion | flops 3145728 | bytes 12582912 | tf_op jit(solution)/shard_map/stack | solution.py:46
  285.6 21.7 %copy.17 = bf16[4,32,2,3,1,4096]{5,0,4,3,2,1:T(4,128)(2,1)} copy(bf16[4,32,2,3,1,4096]{5,3,1,0,4,2:T(4,128)(2,1)} %pad_maximum_fusion) | data formatting | bytes 12582912 | tf_op jit(solution)/shard_map/stack | solution.py:46
  307.3 87.6 %all_to_all.15 = bf16[4,32,2,3,1,4096]{5,0,4,3,2,1:T(4,128)(2,1)S(1)} all-to-all(bf16[4,32,2,3,1,4096]{5,0,4,3,2,1:T(4,128)(2,1)} %copy.17), channel_id=1, replica_groups=mesh['dp'=4,'mp'=32] {'mp'}, dimensions={1} | all-to-all | bytes 12582912 | tf_op jit(solution)/shard_map/all_to_all | solution.py:96
  394.9 6.1 copy.18
  401.2 7.5 %fusion.120 = f32[384,384]{1,0:T(8,128)S(1)} fusion(bf16[384,4096]{1,0:T(8,128)(2,1)} %reshape_squeeze.9, s32[4096]{0:T(1024)S(1)} %add_multiply_fusion.2, s32[]{:T(128)S(6)} %xor.269, s32[384]{0:T(512)S(1)} %iota_add_fusion, bf16[2,4096,384]{2,1,0:T(8,128)(2,1)} %param.12), kind=kOutput, calls=%fused_computation.152 | convolution fusion | flops 1239416832 | bytes 6899204 | tf_op jit(solution)/shard_map/dot_general | solution.py:36
  408.7 15.5 %convolution_convert_fusion = bf16[384,4096]{1,0:T(8,128)(2,1)} fusion(s32[384]{0:T(512)S(1)} %get-tuple-element.9, s32[]{:T(128)S(6)} %xor.269, bf16[2,384,4096]{2,1,0:T(8,128)(2,1)} %param.14, bf16[384,4096]{1,0:T(8,128)(2,1)} %reshape_squeeze.9, s32[4096]{0:T(1024)S(1)} %add_multiply_fusion.2, s32[384]{0:T(512)S(1)} %iota_add_fusion, ...), kind=kOutput, calls=%fused_computation.90 | convolution fusion | flops 2484436992 | bytes 13193216 | tf_op jit(solution)/shard_map/dot_general | solution.py:40
  424.2 7.1 %stack_reshape_stack.15 = bf16[4,32,1,3,1,4096]{5,3,1,0,4,2:T(4,128)(2,1)} reshape(bf16[384,4096]{1,0:T(8,128)(2,1)} %convolution_convert_fusion) | data formatting | bytes 6291456 | tf_op jit(solution)/shard_map/stack;reshape;stack | solution.py:46
  431.3 7.6 %fusion.112 = f32[384,384]{1,0:T(8,128)S(1)} fusion(bf16[384,4096]{1,0:T(8,128)(2,1)} %reshape_squeeze.8, s32[]{:T(128)S(6)} %xor.269, s32[384]{0:T(512)S(1)} %iota_add_fusion, s32[4096]{0:T(1024)S(1)} %add_multiply_fusion.3, bf16[2,4096,384]{2,1,0:T(8,128)(2,1)} %param.12), kind=kOutput, calls=%fused_computation.148 | convolution fusion | flops 1239416832 | bytes 6899204 | tf_op jit(solution)/shard_map/dot_general | solution.py:36
  438.9 15.9 %convolution_convert_fusion.1 = bf16[384,4096]{1,0:T(8,128)(2,1)} fusion(s32[]{:T(128)S(6)} %xor.269, s32[384]{0:T(512)S(1)} %get-tuple-element.10, bf16[2,384,4096]{2,1,0:T(8,128)(2,1)} %param.14, bf16[384,4096]{1,0:T(8,128)(2,1)} %reshape_squeeze.8, s32[384]{0:T(512)S(1)} %iota_add_fusion, s32[4096]{0:T(1024)S(1)} %add_multiply_fusion.3, ...), kind=kOutput, calls=%fused_computation.91 | convolution fusion | flops 2484436992 | bytes 13193216 | tf_op jit(solution)/shard_map/dot_general | solution.py:40
  454.8 7.1 %stack_reshape_stack.14 = bf16[4,32,1,3,1,4096]{5,3,1,0,4,2:T(4,128)(2,1)} reshape(bf16[384,4096]{1,0:T(8,128)(2,1)} %convolution_convert_fusion.1) | data formatting | bytes 6291456 | tf_op jit(solution)/shard_map/stack;reshape;stack | solution.py:46
  461.9 8.8 %pad_maximum_fusion.1 = bf16[4,32,2,3,1,4096]{5,3,1,0,4,2:T(4,128)(2,1)} fusion(bf16[4,32,1,3,1,4096]{5,3,1,0,4,2:T(4,128)(2,1)} %stack_reshape_stack.15, bf16[4,32,1,3,1,4096]{5,3,1,0,4,2:T(4,128)(2,1)} %stack_reshape_stack.14), kind=kLoop, calls=%fused_computation.21 | loop fusion | flops 3145728 | bytes 12582912 | tf_op jit(solution)/shard_map/stack | solution.py:46
  470.6 21.3 %copy.20 = bf16[4,32,2,3,1,4096]{5,0,4,3,2,1:T(4,128)(2,1)} copy(bf16[4,32,2,3,1,4096]{5,3,1,0,4,2:T(4,128)(2,1)} %pad_maximum_fusion.1) | data formatting | bytes 12582912 | tf_op jit(solution)/shard_map/stack | solution.py:46
  492.0 78.0 %all_to_all.16 = bf16[4,32,2,3,1,4096]{5,0,4,3,2,1:T(4,128)(2,1)S(1)} all-to-all(bf16[4,32,2,3,1,4096]{5,0,4,3,2,1:T(4,128)(2,1)} %copy.20), channel_id=1, replica_groups=mesh['dp'=4,'mp'=32] {'mp'}, dimensions={1} | all-to-all | bytes 12582912 | tf_op jit(solution)/shard_map/all_to_all | solution.py:96
  569.9 6.1 copy.21
  576.7 4.1 copy.19
  584.1 53.3 %reduce-scatter.5.cloned.1.call-done = bf16[1,32,2,3,1,4096]{5,1,4,3,2,0:T(8,128)(2,1)} async-done(((bf16[4,32,2,3,1,4096]{5,1,4,3,2,0:T(8,128)(2,1)}), bf16[1,32,2,3,1,4096]{5,1,4,3,2,0:T(8,128)(2,1)}) %reduce-scatter.5.cloned.1.call-update) | async-done | bytes 1572880 | tf_op jit(solution)/shard_map/reduce_scatter | solution.py:97
  641.5 4.3 convert_element_type.279
  (39 shorter events, 26.7 us)
Async XLA Ops:
  7.2 3.6 copy-start
  7.2 79.6 %all-gather.2.cloned.1.call-start = ((), (), s32[]{:S(2)}) async-start(), calls=%async_computation.5 | async-start | bytes 7864320 | tf_op jit(solution)/shard_map/all_gather | solution.py:91
  10.2 0.5 copy-start.4
  97.1 85.6 %all-to-all-start = ((bf16[4,32,2,3,4096]{4,0,3,2,1:T(4,128)(2,1)}), bf16[4,32,2,3,4096]{4,0,3,2,1:T(4,128)(2,1)}, u32[]{:S(2)}, u32[]{:S(2)}) async-start(bf16[4,32,2,3,4096]{4,0,3,2,1:T(4,128)(2,1)} %copy.14), calls=%async_computation | async-start | bytes 12582912 | tf_op jit(solution)/shard_map/all_to_all | solution.py:92
  104.7 471.9 %reduce-scatter.3.cloned.1.call-start = ((), (), s32[]{:S(2)}) async-start(), calls=%async_computation.6 | async-start | bytes 7864320 | tf_op jit(solution)/shard_map/reduce_scatter | solution.py:97
  401.1 236.3 %reduce-scatter.5.cloned.1.call-start = ((), (), s32[]{:S(2)}) async-start(), calls=%async_computation.7 | async-start | bytes 7864320 | tf_op jit(solution)/shard_map/reduce_scatter | solution.py:97
  576.0 0.6 copy-start.5
  645.8 8.0 %copy-start.1 = (bf16[128,4096]{1,0:T(8,128)(2,1)S(1)}, bf16[128,4096]{1,0:T(8,128)(2,1)}, u32[]{:S(2)}) copy-start(bf16[128,4096]{1,0:T(8,128)(2,1)} %param.9) | copy-start | bytes 3145732
  648.0 3.9 copy-start.2
  648.0 3.9 copy-start.3
  648.0 3.9 copy-start.6
Sparse Core Ops, SparseCore 0:
  17.7 69.0 all-gather.1
  401.2 61.1 reduce-scatter.2
  576.2 61.2 reduce-scatter.4
where the time goes:
time: 668 us; the launch traced here: 661 us
  waiting for transfers between devices  200 us (30%)
  blocking collectives  166 us (25%)
  local copies, waits for them, and re-layouts  156 us (23%)
  matrix products  94.5 us (14%)
  other arithmetic  22.4 us (3%)
  between operations  14.8 us (2%)
  starting transfers between devices  7.92 us (1%)
    all_to_all x2, blocking collectives, finish(): lax.all_to_all(partials, 'mp', split_axis=1, concat_axis=1, tiled=True)  166 us
    all_to_all x1, waiting for transfers between devices, shards(): lax.all_to_all(grouped, 'mp', split_axis=1, concat_axis=1, tiled=True)  77 us
    another operation x6, local copies, waits for them, and re-layouts, expert_rows(): return jnp.stack(per_expert, axis=2)  71.4 us
    all_gather x1, waiting for transfers between devices, shards(): grouped = lax.all_gather(outgoing[None], 'dp', axis=0, tiled=True)  69.3 us
    dot_general x4, matrix products, expert_rows(): jnp.dot(hidden, down_moved, preferred_element_type=jnp.float32)  62.6 us
    reduce_scatter x2, waiting for transfers between devices, finish(): lax.psum_scatter(returned.astype(jnp.float32).astype(jnp.bfloat16), 'dp',...  53.4 us
    dot_general x4, matrix products, expert_rows(): jnp.dot(flat_rows, gate_moved, preferred_element_type=jnp.float32)  30.1 us
    slice x3, local copies, waits for them, and re-layouts, expert_rows(): flat_rows = arrived[:, :, local_expert].reshape(-1, model_width)  19 us
  transfers between devices with their start and end apart: 4, of which 3 were waited for; matrix products, arithmetic and copies ran while one was open for 16% of the time, Pallas kernels for 0%

commit v1 on v0

--- a/solution.py
+++ b/solution.py
@@ -88,7 +88,9 @@
         selector.astype(jnp.bfloat16), tokens, preferred_element_type=jnp.float32
     ).astype(jnp.bfloat16)
     outgoing = outgoing.reshape(mp_count, local_count, capacity, model_width)
-    grouped = lax.all_gather(outgoing[None], "dp", axis=0, tiled=True)
+    grouped = jnp.concatenate(
+        lax.all_to_all(jnp.stack([outgoing[None]] * lax.axis_size("dp")), "dp", 0, 0), axis=0
+    )
     arrived = lax.all_to_all(grouped, "mp", split_axis=1, concat_axis=1, tiled=True)
 
     def finish(weight_sets):

time: 668 us -> 676 us (1.012)
  blocking collectives: 166 us -> 241 us
  waiting for transfers between devices: 200 us -> 130 us
    all_to_all x0 -> x1, blocking collectives: none -> 76.1 us  [shards(): lax.all_to_all(jnp.stack([outgoing[None]] * lax.axis_size('dp')), 'dp', 0...]
    all_gather x1 -> x0, waiting for transfers between devices: 69.3 us -> none  [shards(): grouped = lax.all_gather(outgoing[None], 'dp', axis=0, tiled=True)]
    all_gather x1 -> x0, local copies, waits for them, and re-layouts: 10.3 us -> none  [shards(): grouped = lax.all_gather(outgoing[None], 'dp', axis=0, tiled=True)]
    reshape x0 -> x1, local copies, waits for them, and re-layouts: none -> 10.3 us  [shards(): jnp.concatenate(lax.all_to_all(jnp.stack([outgoing[None]] * lax.axis_size...]
  transfers between devices with their start and end apart: 4 -> 3, of which waited for: 3 -> 2; matrix products, arithmetic and copies ran while one was open for 16% -> 16% of each run, Pallas kernels for 0% -> 0%
where the time goes in v1:
time: 676 us; the launch traced here: 667 us
  blocking collectives  241 us (36%)
  local copies, waits for them, and re-layouts  155 us (23%)
  waiting for transfers between devices  130 us (19%)
  matrix products  94.4 us (14%)
  other arithmetic  22.4 us (3%)
  between operations  15.1 us (2%)
  starting transfers between devices  9.26 us (1%)
    all_to_all x2, blocking collectives, finish(): lax.all_to_all(partials, 'mp', split_axis=1, concat_axis=1, tiled=True)  165 us
    all_to_all x1, waiting for transfers between devices, shards(): lax.all_to_all(grouped, 'mp', split_axis=1, concat_axis=1, tiled=True)  77 us
    all_to_all x1, blocking collectives, shards(): lax.all_to_all(jnp.stack([outgoing[None]] * lax.axis_size('dp')), 'dp', 0...  76.1 us
    another operation x6, local copies, waits for them, and re-layouts, expert_rows(): return jnp.stack(per_expert, axis=2)  71.3 us
    dot_general x4, matrix products, expert_rows(): jnp.dot(hidden, down_moved, preferred_element_type=jnp.float32)  62.7 us
    reduce_scatter x2, waiting for transfers between devices, finish(): lax.psum_scatter(returned.astype(jnp.float32).astype(jnp.bfloat16), 'dp',...  52.5 us
    dot_general x4, matrix products, expert_rows(): jnp.dot(flat_rows, gate_moved, preferred_element_type=jnp.float32)  30 us
    slice x3, local copies, waits for them, and re-layouts, expert_rows(): flat_rows = arrived[:, :, local_expert].reshape(-1, model_width)  18.9 us
  transfers between devices with their start and end apart: 3, of which 2 were waited for; matrix products, arithmetic and copies ran while one was open for 16% of the time, Pallas kernels for 0%

profile of v1, /device:TPU:1, one launch (start us, length us, event | category | flops | bytes accessed | tf_op | source)
XLA Modules:
  0.0 667.5 jit_solution(7669273173260167474)
XLA Ops:
  17.2 76.1 %all_to_all.20 = bf16[4,1,32,2,3,4096]{5,2,4,3,1,0:T(8,128)(2,1)} all-to-all(bf16[4,1,32,2,3,4096]{5,2,4,3,1,0:T(8,128)(2,1)S(1)} %stack.9), channel_id=1, replica_groups=mesh['dp'=4,'mp'=32] {'dp'}, dimensions={0} | all-to-all | bytes 12582912 | tf_op jit(solution)/shard_map/all_to_all | solution.py:92
  93.3 10.3 %copy.15 = bf16[4,32,2,3,4096]{4,0,3,2,1:T(4,128)(2,1)} copy(bf16[4,32,2,3,4096]{4,1,3,2,0:T(8,128)(2,1)} %bitcast.91) | data formatting | bytes 12582912 | tf_op jit(solution)/shard_map/reshape | solution.py:91
  103.6 9.0 %all-to-all-start.1 = ((bf16[4,32,2,3,4096]{4,0,3,2,1:T(4,128)(2,1)}), bf16[4,32,2,3,4096]{4,0,3,2,1:T(4,128)(2,1)}, u32[]{:S(2)}, u32[]{:S(2)}) async-start(bf16[4,32,2,3,4096]{4,0,3,2,1:T(4,128)(2,1)} %copy.15), calls=%async_computation.1 | async-start | bytes 12582912 | tf_op jit(solution)/shard_map/all_to_all | solution.py:94
  113.5 77.0 %all-to-all-done.1 = bf16[4,32,2,3,4096]{4,0,3,2,1:T(4,128)(2,1)} async-done(((bf16[4,32,2,3,4096]{4,0,3,2,1:T(4,128)(2,1)}), bf16[4,32,2,3,4096]{4,0,3,2,1:T(4,128)(2,1)}, u32[]{:S(2)}, u32[]{:S(2)}) %all-to-all-start.1) | async-done | bytes 6291488 | tf_op jit(solution)/shard_map/all_to_all | solution.py:94
  190.5 6.9 %fusion.296 = (bf16[4,32,1,3,4096]{4,0,3,2,1:T(4,128)(2,1)}, bf16[4,32,1,3,4096]{4,0,3,2,1:T(4,128)(2,1)S(1)}) fusion(bf16[4,32,2,3,4096]{4,0,3,2,1:T(4,128)(2,1)} %all-to-all-done.1), kind=kLoop, calls=%fused_computation.284 | loop fusion | bytes 12582912 | tf_op jit(solution)/shard_map/slice | solution.py:33
  197.4 4.6 copy.17
  202.1 7.4 %reshape_squeeze.9 = bf16[384,4096]{1,0:T(8,128)(2,1)} reshape(bf16[4,32,1,3,4096]{4,3,1,0,2:T(4,128)(2,1)} %copy.17) | data formatting | bytes 6291456 | tf_op jit(solution)/shard_map/reshape;squeeze | solution.py:33
  209.5 7.5 %fusion.118 = f32[384,384]{1,0:T(8,128)S(1)} fusion(bf16[384,4096]{1,0:T(8,128)(2,1)} %reshape_squeeze.9, s32[4096]{0:T(1024)S(1)} %add_multiply_fusion.2, s32[]{:T(128)S(6)} %xor.269, s32[384]{0:T(512)S(1)} %iota_add_fusion, bf16[2,4096,384]{2,1,0:T(8,128)(2,1)} %param.12), kind=kOutput, calls=%fused_computation.151 | convolution fusion | flops 1239416832 | bytes 6899204 | tf_op jit(solution)/shard_map/dot_general | solution.py:36
  217.0 15.8 %convolution_convert_fusion.2 = bf16[384,4096]{1,0:T(8,128)(2,1)} fusion(s32[384]{0:T(512)S(1)} %get-tuple-element.9, s32[]{:T(128)S(6)} %xor.269, bf16[2,384,4096]{2,1,0:T(8,128)(2,1)} %param.14, bf16[384,4096]{1,0:T(8,128)(2,1)} %reshape_squeeze.9, s32[4096]{0:T(1024)S(1)} %add_multiply_fusion.2, s32[384]{0:T(512)S(1)} %iota_add_fusion, ...), kind=kOutput, calls=%fused_computation.92 | convolution fusion | flops 2484436992 | bytes 13193216 | tf_op jit(solution)/shard_map/dot_general | solution.py:40
  232.7 7.1 %stack_reshape_stack.13 = bf16[4,32,1,3,1,4096]{5,3,1,0,4,2:T(4,128)(2,1)} reshape(bf16[384,4096]{1,0:T(8,128)(2,1)} %convolution_convert_fusion.2) | data formatting | bytes 6291456 | tf_op jit(solution)/shard_map/stack;reshape;stack | solution.py:46
  239.8 7.4 %copy.16 = bf16[4,32,1,3,4096]{4,3,1,0,2:T(4,128)(2,1)} copy(bf16[4,32,1,3,4096]{4,0,3,2,1:T(4,128)(2,1)} %get-tuple-element.5) | data formatting | bytes 6291456 | tf_op jit(solution)/shard_map/slice | solution.py:33
  247.2 7.4 %reshape_squeeze.8 = bf16[384,4096]{1,0:T(8,128)(2,1)} reshape(bf16[4,32,1,3,4096]{4,3,1,0,2:T(4,128)(2,1)} %copy.16) | data formatting | bytes 6291456 | tf_op jit(solution)/shard_map/reshape;squeeze | solution.py:33
  254.6 7.5 %fusion.110 = f32[384,384]{1,0:T(8,128)S(1)} fusion(bf16[384,4096]{1,0:T(8,128)(2,1)} %reshape_squeeze.8, s32[]{:T(128)S(6)} %xor.269, s32[384]{0:T(512)S(1)} %iota_add_fusion, s32[4096]{0:T(1024)S(1)} %add_multiply_fusion.3, bf16[2,4096,384]{2,1,0:T(8,128)(2,1)} %param.12), kind=kOutput, calls=%fused_computation.147 | convolution fusion | flops 1239416832 | bytes 6899204 | tf_op jit(solution)/shard_map/dot_general | solution.py:36
  262.1 15.5 %convolution_convert_fusion.3 = bf16[384,4096]{1,0:T(8,128)(2,1)} fusion(s32[]{:T(128)S(6)} %xor.269, s32[384]{0:T(512)S(1)} %get-tuple-element.10, bf16[2,384,4096]{2,1,0:T(8,128)(2,1)} %param.14, bf16[384,4096]{1,0:T(8,128)(2,1)} %reshape_squeeze.8, s32[384]{0:T(512)S(1)} %iota_add_fusion, s32[4096]{0:T(1024)S(1)} %add_multiply_fusion.3, ...), kind=kOutput, calls=%fused_computation.93 | convolution fusion | flops 2484436992 | bytes 13193216 | tf_op jit(solution)/shard_map/dot_general | solution.py:40
  277.6 7.1 %stack_reshape_stack.12 = bf16[4,32,1,3,1,4096]{5,3,1,0,4,2:T(4,128)(2,1)} reshape(bf16[384,4096]{1,0:T(8,128)(2,1)} %convolution_convert_fusion.3) | data formatting | bytes 6291456 | tf_op jit(solution)/shard_map/stack;reshape;stack | solution.py:46
  284.7 8.7 %pad_maximum_fusion = bf16[4,32,2,3,1,4096]{5,3,1,0,4,2:T(4,128)(2,1)} fusion(bf16[4,32,1,3,1,4096]{5,3,1,0,4,2:T(4,128)(2,1)} %stack_reshape_stack.13, bf16[4,32,1,3,1,4096]{5,3,1,0,4,2:T(4,128)(2,1)} %stack_reshape_stack.12), kind=kLoop, calls=%fused_computation.20 | loop fusion | flops 3145728 | bytes 12582912 | tf_op jit(solution)/shard_map/stack | solution.py:46
  293.4 21.7 %copy.18 = bf16[4,32,2,3,1,4096]{5,0,4,3,2,1:T(4,128)(2,1)} copy(bf16[4,32,2,3,1,4096]{5,3,1,0,4,2:T(4,128)(2,1)} %pad_maximum_fusion) | data formatting | bytes 12582912 | tf_op jit(solution)/shard_map/stack | solution.py:46
  315.1 87.6 %all_to_all.21 = bf16[4,32,2,3,1,4096]{5,0,4,3,2,1:T(4,128)(2,1)S(1)} all-to-all(bf16[4,32,2,3,1,4096]{5,0,4,3,2,1:T(4,128)(2,1)} %copy.18), channel_id=1, replica_groups=mesh['dp'=4,'mp'=32] {'mp'}, dimensions={1} | all-to-all | bytes 12582912 | tf_op jit(solution)/shard_map/all_to_all | solution.py:98
  402.7 6.1 copy.19
  408.9 7.5 %fusion.120 = f32[384,384]{1,0:T(8,128)S(1)} fusion(bf16[384,4096]{1,0:T(8,128)(2,1)} %reshape_squeeze.9, s32[4096]{0:T(1024)S(1)} %add_multiply_fusion.2, s32[]{:T(128)S(6)} %xor.269, s32[384]{0:T(512)S(1)} %iota_add_fusion, bf16[2,4096,384]{2,1,0:T(8,128)(2,1)} %param.12), kind=kOutput, calls=%fused_computation.152 | convolution fusion | flops 1239416832 | bytes 6899204 | tf_op jit(solution)/shard_map/dot_general | solution.py:36
  416.4 15.5 %convolution_convert_fusion = bf16[384,4096]{1,0:T(8,128)(2,1)} fusion(s32[384]{0:T(512)S(1)} %get-tuple-element.9, s32[]{:T(128)S(6)} %xor.269, bf16[2,384,4096]{2,1,0:T(8,128)(2,1)} %param.14, bf16[384,4096]{1,0:T(8,128)(2,1)} %reshape_squeeze.9, s32[4096]{0:T(1024)S(1)} %add_multiply_fusion.2, s32[384]{0:T(512)S(1)} %iota_add_fusion, ...), kind=kOutput, calls=%fused_computation.90 | convolution fusion | flops 2484436992 | bytes 13193216 | tf_op jit(solution)/shard_map/dot_general | solution.py:40
  431.9 7.1 %stack_reshape_stack.15 = bf16[4,32,1,3,1,4096]{5,3,1,0,4,2:T(4,128)(2,1)} reshape(bf16[384,4096]{1,0:T(8,128)(2,1)} %convolution_convert_fusion) | data formatting | bytes 6291456 | tf_op jit(solution)/shard_map/stack;reshape;stack | solution.py:46
  439.0 7.5 %fusion.112 = f32[384,384]{1,0:T(8,128)S(1)} fusion(bf16[384,4096]{1,0:T(8,128)(2,1)} %reshape_squeeze.8, s32[]{:T(128)S(6)} %xor.269, s32[384]{0:T(512)S(1)} %iota_add_fusion, s32[4096]{0:T(1024)S(1)} %add_multiply_fusion.3, bf16[2,4096,384]{2,1,0:T(8,128)(2,1)} %param.12), kind=kOutput, calls=%fused_computation.148 | convolution fusion | flops 1239416832 | bytes 6899204 | tf_op jit(solution)/shard_map/dot_general | solution.py:36
  446.6 15.9 %convolution_convert_fusion.1 = bf16[384,4096]{1,0:T(8,128)(2,1)} fusion(s32[]{:T(128)S(6)} %xor.269, s32[384]{0:T(512)S(1)} %get-tuple-element.10, bf16[2,384,4096]{2,1,0:T(8,128)(2,1)} %param.14, bf16[384,4096]{1,0:T(8,128)(2,1)} %reshape_squeeze.8, s32[384]{0:T(512)S(1)} %iota_add_fusion, s32[4096]{0:T(1024)S(1)} %add_multiply_fusion.3, ...), kind=kOutput, calls=%fused_computation.91 | convolution fusion | flops 2484436992 | bytes 13193216 | tf_op jit(solution)/shard_map/dot_general | solution.py:40
  462.4 7.1 %stack_reshape_stack.14 = bf16[4,32,1,3,1,4096]{5,3,1,0,4,2:T(4,128)(2,1)} reshape(bf16[384,4096]{1,0:T(8,128)(2,1)} %convolution_convert_fusion.1) | data formatting | bytes 6291456 | tf_op jit(solution)/shard_map/stack;reshape;stack | solution.py:46
  469.5 8.7 %pad_maximum_fusion.1 = bf16[4,32,2,3,1,4096]{5,3,1,0,4,2:T(4,128)(2,1)} fusion(bf16[4,32,1,3,1,4096]{5,3,1,0,4,2:T(4,128)(2,1)} %stack_reshape_stack.15, bf16[4,32,1,3,1,4096]{5,3,1,0,4,2:T(4,128)(2,1)} %stack_reshape_stack.14), kind=kLoop, calls=%fused_computation.21 | loop fusion | flops 3145728 | bytes 12582912 | tf_op jit(solution)/shard_map/stack | solution.py:46
  478.2 21.3 %copy.21 = bf16[4,32,2,3,1,4096]{5,0,4,3,2,1:T(4,128)(2,1)} copy(bf16[4,32,2,3,1,4096]{5,3,1,0,4,2:T(4,128)(2,1)} %pad_maximum_fusion.1) | data formatting | bytes 12582912 | tf_op jit(solution)/shard_map/stack | solution.py:46
  499.5 77.7 %all_to_all.22 = bf16[4,32,2,3,1,4096]{5,0,4,3,2,1:T(4,128)(2,1)S(1)} all-to-all(bf16[4,32,2,3,1,4096]{5,0,4,3,2,1:T(4,128)(2,1)} %copy.21), channel_id=1, replica_groups=mesh['dp'=4,'mp'=32] {'mp'}, dimensions={1} | all-to-all | bytes 12582912 | tf_op jit(solution)/shard_map/all_to_all | solution.py:98
  577.3 6.1 copy.22
  584.1 4.1 copy.20
  591.6 52.5 %reduce-scatter.5.cloned.1.call-done = bf16[1,32,2,3,1,4096]{5,1,4,3,2,0:T(8,128)(2,1)} async-done(((bf16[4,32,2,3,1,4096]{5,1,4,3,2,0:T(8,128)(2,1)}), bf16[1,32,2,3,1,4096]{5,1,4,3,2,0:T(8,128)(2,1)}) %reduce-scatter.5.cloned.1.call-update) | async-done | bytes 1572880 | tf_op jit(solution)/shard_map/reduce_scatter | solution.py:99
  648.1 4.3 convert_element_type.279
  (38 shorter events, 26.4 us)
Async XLA Ops:
  7.2 3.6 copy-start
  10.2 0.6 copy-start.4
  103.6 87.0 %all-to-all-start.1 = ((bf16[4,32,2,3,4096]{4,0,3,2,1:T(4,128)(2,1)}), bf16[4,32,2,3,4096]{4,0,3,2,1:T(4,128)(2,1)}, u32[]{:S(2)}, u32[]{:S(2)}) async-start(bf16[4,32,2,3,4096]{4,0,3,2,1:T(4,128)(2,1)} %copy.15), calls=%async_computation.1 | async-start | bytes 12582912 | tf_op jit(solution)/shard_map/all_to_all | solution.py:94
  112.6 471.5 %reduce-scatter.3.cloned.1.call-start = ((), (), s32[]{:S(2)}) async-start(), calls=%async_computation.6 | async-start | bytes 7864320 | tf_op jit(solution)/shard_map/reduce_scatter | solution.py:99
  408.9 235.2 %reduce-scatter.5.cloned.1.call-start = ((), (), s32[]{:S(2)}) async-start(), calls=%async_computation.7 | async-start | bytes 7864320 | tf_op jit(solution)/shard_map/reduce_scatter | solution.py:99
  583.4 0.7 copy-start.5
  652.4 8.0 %copy-start.1 = (bf16[128,4096]{1,0:T(8,128)(2,1)S(1)}, bf16[128,4096]{1,0:T(8,128)(2,1)}, u32[]{:S(2)}) copy-start(bf16[128,4096]{1,0:T(8,128)(2,1)} %param.9) | copy-start | bytes 3145732
  654.6 3.9 copy-start.2
  654.6 3.9 copy-start.3
  654.6 3.9 copy-start.6
Sparse Core Ops, SparseCore 0:
  409.0 59.9 reduce-scatter.2
  583.5 60.4 reduce-scatter.4
